TPU v7x, 32 devices: a whole 2x2x4 slice. The times are simulated.
32 devices in a mesh: groups: 2 (over y), batch: 4 (over z), heads: 4 (over x, core).
Axes of the slice: x: 2, y: 2, z: 4, core: 2. Of those that a mesh axis runs over, the one named last changes fastest.
Arguments:
- tokens: bfloat16 [768, 4096], P(('groups', 'batch')), parts along dimension 0, may hold values from -6 to 6
- query_weight: bfloat16 [16, 4096, 128], P('heads', 'batch'), may hold values from -0.09375 to 0.09375
- keys: bfloat16 [4, 768, 128], P('heads', ('groups', 'batch')), parts along dimension 1, may hold values from -48 to 48
- values: bfloat16 [4, 768, 128], P('heads', ('groups', 'batch')), parts along dimension 1, may hold values from -6 to 6
- segment_ids: int32 [768], P(('groups', 'batch')), parts along dimension 0, may hold values from 0 to 1, as said below
- out_weight: bfloat16 [16, 4096, 128], P('heads', 'batch'), may hold values from -1.5 to 1.5
Outputs:
- mixed: bfloat16 [768, 4096], P(('groups', 'batch'), 'heads'), parts along dimension 0
There are 2 independent parts, one for each index of `groups`. A program takes and returns all parts, laid end to end along the dimension named above; an argument that names none is the same for every part. Nothing has to cross between parts.
Inputs may be any that keep to these rules, and one draw needn't show every extreme that they name: `segment_ids`: two sequences in token order, each of at least 96 tokens.
All inputs are finite; a program needn't handle non-finite values.
Results may differ from a plain program's by a relative error of at most 0.0086.
Values may be sent and summed in bfloat16 or wider, within the bound.
A program may use at most 64 MiB of HBM per device.

v0:
```python
import jax
import jax.numpy as jnp
from jax import lax
from jax.sharding import PartitionSpec as P


def on_device(tokens, query_weight, keys, values, segment_ids, out_weight):
    rows = tokens.shape[0]
    head_size = query_weight.shape[2]
    local_heads = query_weight.shape[0]
    kv_local = keys.shape[0]
    sharing = local_heads // kv_local
    first = lax.axis_index("batch") * rows
    places = first + jnp.arange(rows, dtype=jnp.int32)
    query_places = jnp.tile(places, sharing)
    query_segments = jnp.tile(segment_ids, sharing)
    query = jnp.einsum(
        "tc,hcd->htd",
        tokens,
        lax.all_gather(query_weight, "batch", axis=1, tiled=True),
        preferred_element_type=jnp.float32,
    ).astype(jnp.bfloat16)
    query = query.reshape(kv_local, sharing * rows, head_size)
    factor = 1.0 / jnp.sqrt(jnp.float32(head_size))
    begin = (
        jnp.full((kv_local, sharing * rows), -1e30, jnp.float32),
        jnp.zeros((kv_local, sharing * rows), jnp.float32),
        jnp.zeros((kv_local, sharing * rows, head_size), jnp.float32),
    )
    key_piece = lax.all_gather(keys, "batch", axis=1, tiled=True)
    value_piece = lax.all_gather(values, "batch", axis=1, tiled=True)
    segment_piece = lax.all_gather(segment_ids[None, :], "batch", axis=1, tiled=True)
    count = key_piece.shape[1]
    width = 4
    block = width * rows

    def inner(state, number):
        running, total, gathered = state
        offset = number * block
        key_block = lax.dynamic_slice_in_dim(key_piece, offset, block, 1)
        value_block = lax.dynamic_slice_in_dim(value_piece, offset, block, 1)
        segment_block = lax.dynamic_slice_in_dim(segment_piece[0], offset, block, 0)
        scores = (
            jnp.einsum("gqd,gkd->gqk", query, key_block, preferred_element_type=jnp.float32)
            * factor
        )
        key_places = offset + jnp.arange(block, dtype=jnp.int32)
        keep = (segment_block[None, :] == query_segments[:, None]) & (
            key_places[None, :] <= query_places[:, None]
        )
        block_top = jnp.max(jnp.where(keep[None], scores, jnp.float32(-1e30)), axis=2)
        newer = jnp.maximum(running, block_top)
        weights = jnp.where(keep[None], jnp.exp(scores - newer[:, :, None]), jnp.float32(0.0))
        shrink = jnp.exp(running - newer)
        total = total * shrink + jnp.sum(weights, axis=2)
        gathered = gathered * shrink[:, :, None] + jnp.einsum(
            "gqk,gkd->gqd",
            weights,
            value_block.astype(jnp.float32),
            precision=lax.Precision.HIGHEST,
        )
        return ((newer, total, gathered), None)

    result, unused = lax.scan(inner, begin, jnp.arange(count // block, dtype=jnp.int32))
    running, total, gathered = result
    attended = (
        (gathered / total[:, :, None]).astype(jnp.bfloat16).reshape(local_heads, rows, head_size)
    )
    terms = jnp.einsum(
        "htd,hcd->tc",
        attended,
        lax.all_gather(out_weight, "batch", axis=1, tiled=True),
        preferred_element_type=jnp.float32,
    )
    return lax.psum_scatter(terms, "heads", scatter_dimension=1, tiled=True).astype(jnp.bfloat16)


def solution(mesh):
    return jax.shard_map(
        on_device,
        mesh=mesh,
        in_specs=(
            P(("groups", "batch"), None),
            P("heads", "batch", None),
            P("heads", ("groups", "batch"), None),
            P("heads", ("groups", "batch"), None),
            P(("groups", "batch")),
            P("heads", "batch", None),
        ),
        out_specs=P(("groups", "batch"), "heads"),
        check_vma=False,
    )
```

profile of v0, /device:TPU:2, one launch (start us, length us, event | category | flops | bytes accessed | tf_op | source)
XLA Modules:
  0.0 213.6 jit_solution(13592401438096764603)
XLA Ops:
  6.5 0.0 copy-start
  6.5 0.0 all-gather.4.cloned.1.call-start
  6.5 0.7 all-gather.4.cloned.1.call-update
  7.3 0.0 all-gather.6.cloned.1.call-start
  7.3 0.7 all-gather.6.cloned.1.call-update
  8.0 0.0 reduce-scatter.2.cloned.1.call-start
  8.1 0.1 le.23
  8.2 0.7 tile.4
  8.8 0.1 eq.26
  8.9 1.2 dynamic-slice
  10.8 0.9 dynamic-update-slice
  11.7 8.4 %all-reduce = s32[384]{0:T(512)S(1)} all-reduce(s32[384]{0:T(512)S(1)} %dynamic-update-slice), channel_id=2, replica_groups=mesh['groups'=2,'batch'=4,'heads'=4] {'batch'}, use_global_device_ids=true, to_apply=%add | all-reduce | flops 384 | bytes 3072
  20.1 14.1 %all_gather.17 = bf16[1,384,128]{2,1,0:T(8,128)(2,1)S(1)} all-gather(bf16[1,96,128]{2,1,0:T(8,128)(2,1)} %param.8), channel_id=1, replica_groups=mesh['groups'=2,'batch'=4,'heads'=4] {'batch'}, dimensions={1}, use_global_device_ids=true | all-gather | bytes 122880 | tf_op jit(solution)/shard_map/all_gather | solution.py:30
  34.2 14.7 %all_gather.18 = bf16[1,384,128]{2,1,0:T(8,128)(2,1)S(1)} all-gather(bf16[1,96,128]{2,1,0:T(8,128)(2,1)} %param.9), channel_id=1, replica_groups=mesh['groups'=2,'batch'=4,'heads'=4] {'batch'}, dimensions={1}, use_global_device_ids=true | all-gather | bytes 122880 | tf_op jit(solution)/shard_map/all_gather | solution.py:31
  48.9 44.9 %all-gather.4.cloned.1.call-done = bf16[4,4096,128]{2,1,0:T(8,128)(2,1)} async-done(((bf16[4,1024,128]{2,1,0:T(8,128)(2,1)}), bf16[4,4096,128]{2,1,0:T(8,128)(2,1)}) %all-gather.4.cloned.1.call-update) | async-done | bytes 4194320 | tf_op jit(solution)/shard_map/all_gather | solution.py:20
  93.8 3.0 %convolution_convert_fusion = bf16[4,128,96]{1,2,0:T(8,128)(2,1)S(1)} fusion(bf16[4,4096,128]{2,1,0:T(8,128)(2,1)} %all-gather.4.cloned.1.call-done, bf16[96,4096]{1,0:T(8,128)(2,1)S(1)} %copy-done), kind=kOutput, calls=%fused_computation.5 | convolution fusion | flops 402702336 | bytes 5079040 | tf_op jit(solution)/shard_map/tc,hcd->htd/dot_general | solution.py:17
  96.8 0.3 select_reduce_fusion
  97.1 0.2 fusion.4
  97.4 0.8 fusion.1
  98.1 76.7 %all-gather.6.cloned.1.call-done = bf16[4,4096,128]{2,1,0:T(8,128)(2,1)} async-done(((bf16[4,1024,128]{2,1,0:T(8,128)(2,1)}), bf16[4,4096,128]{2,1,0:T(8,128)(2,1)}) %all-gather.6.cloned.1.call-update) | async-done | bytes 4194320 | tf_op jit(solution)/shard_map/all_gather | solution.py:72
  174.9 4.7 %convolution_bitcast_fusion = f32[96,4096]{1,0:T(8,128)} fusion(bf16[4,96,128]{2,1,0:T(8,128)(2,1)S(1)} %bitcast.23, bf16[4,4096,128]{2,1,0:T(8,128)(2,1)} %all-gather.6.cloned.1.call-done), kind=kOutput, calls=%fused_computation | convolution fusion | flops 402653184 | bytes 5865472 | tf_op jit(solution)/shard_map/htd,hcd->tc/dot_general | solution.py:69
  179.6 0.0 reduce-scatter.2.cloned.1.call-update
  179.6 25.7 %reduce-scatter.2.cloned.1.call-done = f32[96,1024]{1,0:T(8,128)} async-done(((f32[96,4096]{1,0:T(8,128)}), f32[96,1024]{1,0:T(8,128)}) %reduce-scatter.2.cloned.1.call-update) | async-done | bytes 393232 | tf_op jit(solution)/shard_map/reduce_scatter | solution.py:75
  205.3 1.7 convert_element_type.18
  (6 shorter events, 0.0 us)
Async XLA Ops:
  6.5 87.3 %copy-start = (bf16[96,4096]{1,0:T(8,128)(2,1)S(1)}, bf16[96,4096]{1,0:T(8,128)(2,1)}, u32[]{:S(2)}) copy-start(bf16[96,4096]{1,0:T(8,128)(2,1)} %param.6) | copy-start | bytes 2359300
  6.5 87.3 %all-gather.4.cloned.1.call-start = ((), (), s32[]{:S(2)}) async-start(), calls=%async_computation.1 | async-start | bytes 5242880 | tf_op jit(solution)/shard_map/all_gather | solution.py:20
  7.3 167.6 %all-gather.6.cloned.1.call-start = ((), (), s32[]{:S(2)}) async-start(), calls=%async_computation.2 | async-start | bytes 5242880 | tf_op jit(solution)/shard_map/all_gather | solution.py:72
  8.0 197.3 %reduce-scatter.2.cloned.1.call-start = ((), (), s32[]{:S(2)}) async-start(), calls=%async_computation.3 | async-start | bytes 1966080 | tf_op jit(solution)/shard_map/reduce_scatter | solution.py:75
Sparse Core Ops, SparseCore 0:
  8.9 84.8 all-gather.3
  95.4 79.4 all-gather.5
  179.8 25.5 reduce-scatter.1
where the time goes:
time: 217 us; the launch traced here: 214 us
  waiting for transfers between devices  149 us (69%)
  blocking collectives  37.3 us (17%)
  between operations  13.8 us (6%)
  matrix products  8.79 us (4%)
  local copies, waits for them, and re-layouts  2.93 us (1%)
    all_gather x1, waiting for transfers between devices, on_device(): lax.all_gather(out_weight, 'batch', axis=1, tiled=True)  76.7 us
    all_gather x1, waiting for transfers between devices, on_device(): lax.all_gather(query_weight, 'batch', axis=1, tiled=True)  44.9 us
    reduce_scatter x1, waiting for transfers between devices, on_device(): lax.psum_scatter(terms, 'heads', scatter_dimension=1, tiled=True)  25.7 us
    all_gather x1, blocking collectives, on_device(): value_piece = lax.all_gather(values, 'batch', axis=1, tiled=True)  14.7 us
    all_gather x1, blocking collectives, on_device(): key_piece = lax.all_gather(keys, 'batch', axis=1, tiled=True)  14.1 us
    unnamed x1, blocking collectives  8.44 us
    dot_general x1, matrix products, on_device(): jnp.einsum('htd,hcd->tc', attended, lax.all_gather(out_weight, 'batch', a...  4.74 us
  transfers between devices with their start and end apart: 3, of which 3 were waited for; matrix products, arithmetic and copies ran while one was open for 3% of the time, Pallas kernels for 0%

commit v1 on v0

--- a/solution.py
+++ b/solution.py
@@ -1,10 +1,386 @@
+import functools
+
 import jax
 import jax.numpy as jnp
 from jax import lax
+from jax.experimental import pallas as pl
+from jax.experimental.pallas import tpu as pltpu
 from jax.sharding import PartitionSpec as P
 
-
-def on_device(tokens, query_weight, keys, values, segment_ids, out_weight):
+MESH = pl.DeviceIdType.MESH
+
+
+def flip(index, mask):
+    bit = 1
+    while bit <= mask:
+        if mask & bit:
+            index = index + bit - 2 * bit * lax.rem(lax.div(index, bit), 2)
+        bit *= 2
+    return index
+
+
+def kernel(
+    tokens,
+    query_weight,
+    keys,
+    values,
+    segments,
+    out_weight,
+    out,
+    w_query,
+    w_out,
+    token_block,
+    partial_out,
+    partial_in,
+    key_all,
+    value_all,
+    segment_all,
+    attended_all,
+    core_out,
+    core_in,
+    chip_out,
+    chip_in,
+    final,
+    load_sem,
+    token_send,
+    token_recv,
+    share_send,
+    share_recv,
+    key_send,
+    key_recv,
+    value_send,
+    value_recv,
+    segment_send,
+    segment_recv,
+    partial_send,
+    partial_recv,
+    attended_send,
+    attended_recv,
+    core_send,
+    core_recv,
+    chip_send,
+    chip_recv,
+    final_send,
+    final_recv,
+):
+    rows, model = tokens.shape
+    local_heads, depth, head_size = query_weight.shape
+    wide = local_heads * head_size
+    plane = lax.axis_index("batch")
+    head = lax.axis_index("heads")
+    others = (1, 2, 3)
+    bf16, f32 = jnp.bfloat16, jnp.float32
+
+    def remote(src, dst, send, recv, **device):
+        return pltpu.make_async_remote_copy(
+            src_ref=src,
+            dst_ref=dst,
+            send_sem=send,
+            recv_sem=recv,
+            device_id=device,
+            device_id_type=MESH,
+        )
+
+    own_tokens = pltpu.make_async_copy(
+        tokens.at[:, pl.ds(pl.multiple_of(plane * depth, depth), depth)],
+        token_block.at[0],
+        load_sem.at[0],
+    )
+    own_keys = pltpu.make_async_copy(keys.at[0], key_all.at[plane], load_sem.at[1])
+    own_values = pltpu.make_async_copy(values.at[0], value_all.at[plane], load_sem.at[2])
+    query_loads = [
+        pltpu.make_async_copy(
+            query_weight.at[i], w_query.at[:, pl.ds(i * head_size, head_size)], load_sem.at[3 + i]
+        )
+        for i in range(local_heads)
+    ]
+    out_loads = [
+        pltpu.make_async_copy(
+            out_weight.at[i],
+            w_out.at[:, pl.ds(i * head_size, head_size)],
+            load_sem.at[3 + local_heads + i],
+        )
+        for i in range(local_heads)
+    ]
+    for load in [*query_loads, own_tokens, own_keys, own_values, *out_loads]:
+        load.start()
+    segment_all[plane] = jnp.zeros(segment_all.shape[1:], jnp.int32)
+    segment_all[plane, 0:1, 0:rows] = segments[...]
+
+    barrier = pltpu.get_barrier_semaphore()
+    for d in others:
+        pl.semaphore_signal(
+            barrier, inc=1, device_id={"batch": flip(plane, d)}, device_id_type=MESH
+        )
+        pl.semaphore_signal(barrier, inc=1, device_id={"heads": flip(head, d)}, device_id_type=MESH)
+
+    @pl.when(plane != head)
+    def _():
+        pl.semaphore_signal(
+            barrier, inc=1, device_id={"batch": head, "heads": plane}, device_id_type=MESH
+        )
+        pl.semaphore_wait(barrier, 2 * len(others) + 1)
+
+    @pl.when(plane == head)
+    def _():
+        pl.semaphore_wait(barrier, 2 * len(others))
+
+    share = depth // (1 + len(SHARE))
+    my_share = lax.rem(head, 1 + len(SHARE))
+    token_copies, share_copies, key_copies, value_copies, segment_copies = {}, {}, {}, {}, {}
+    mine = pl.ds(pl.multiple_of(my_share * share, share), share)
+    for d in (2, 3, 1):
+        peer = flip(plane, d)
+        token_copies[d] = remote(
+            tokens.at[:, pl.ds(pl.multiple_of(peer * depth + my_share * share, share), share)],
+            token_block.at[d, :, mine],
+            token_send.at[d],
+            token_recv.at[d],
+            batch=peer,
+        )
+        token_copies[d].start()
+
+    own_keys.wait()
+    own_values.wait()
+
+    def send_keys():
+        for d in others:
+            peer = flip(plane, d)
+            key_copies[d] = remote(
+                key_all.at[plane], key_all.at[plane], key_send.at[d], key_recv.at[d], batch=peer
+            )
+            value_copies[d] = remote(
+                value_all.at[plane],
+                value_all.at[plane],
+                value_send.at[d],
+                value_recv.at[d],
+                batch=peer,
+            )
+            segment_copies[d] = remote(
+                segment_all.at[plane],
+                segment_all.at[plane],
+                segment_send.at[d],
+                segment_recv.at[d],
+                batch=peer,
+            )
+            for copy in (key_copies[d], value_copies[d], segment_copies[d]):
+                copy.start()
+
+    for load in query_loads:
+        load.wait()
+    own_tokens.wait()
+    query = jnp.dot(token_block[0], w_query[...], preferred_element_type=f32)
+
+    def forward(d):
+        token_copies[d].wait_recv()
+        for s, mask in enumerate(SHARE):
+            share_copies[d, s] = remote(
+                token_block.at[d, :, mine],
+                token_block.at[d, :, mine],
+                share_send.at[d, s],
+                share_recv.at[d, s],
+                heads=flip(head, mask),
+            )
+            share_copies[d, s].start()
+
+    partial_copies = {}
+    forward(1)
+    forward(2)
+    for d in others:
+        for s in range(len(SHARE)):
+            share_copies[d, s].wait_recv()
+        if d == 1:
+            forward(3)
+        partial_out[d] = jnp.dot(token_block[d], w_query[...], preferred_element_type=f32).astype(
+            bf16
+        )
+        partial_copies[d] = remote(
+            partial_out.at[d],
+            partial_in.at[d],
+            partial_send.at[d],
+            partial_recv.at[d],
+            batch=flip(plane, d),
+        )
+        partial_copies[d].start()
+        if d == 1:
+            send_keys()
+
+    for d in others:
+        segment_copies[d].wait_recv()
+    count = segment_all.shape[0]
+    row_at = lax.broadcasted_iota(jnp.int32, (rows, rows), 0)
+    column_at = lax.broadcasted_iota(jnp.int32, (rows, rows), 1)
+    own = segment_all[plane, 0:1, 0:rows]
+    row_segment = jnp.sum(
+        jnp.where(row_at == column_at, jnp.broadcast_to(own, (rows, rows)), 0),
+        axis=1,
+        keepdims=True,
+    )
+    segment_row = jnp.concatenate([segment_all[p, 0:1, 0:rows] for p in range(count)], axis=1)
+    places = lax.broadcasted_iota(jnp.int32, (rows, count * rows), 1)
+    row_places = lax.broadcasted_iota(jnp.int32, (rows, count * rows), 0) + plane * rows
+    keep = (segment_row == row_segment) & (places <= row_places)
+
+    for d in others:
+        key_copies[d].wait_recv()
+        value_copies[d].wait_recv()
+    key_block = jnp.concatenate([key_all[p] for p in range(count)], axis=0)
+    value_block = jnp.concatenate([value_all[p] for p in range(count)], axis=0)
+    for d in others:
+        partial_copies[d].wait_recv()
+        query = query + partial_in[d].astype(f32)
+    query = query.astype(bf16)
+    factor = 1.0 / (head_size**0.5)
+    attended = []
+    for i in range(local_heads):
+        scores = (
+            lax.dot_general(
+                query[:, i * head_size : (i + 1) * head_size],
+                key_block,
+                (((1,), (1,)), ((), ())),
+                preferred_element_type=f32,
+            )
+            * factor
+        )
+        top = jnp.max(jnp.where(keep, scores, -1e30), axis=1, keepdims=True)
+        weights = jnp.where(keep, jnp.exp(scores - top), 0.0)
+        total = jnp.sum(weights, axis=1, keepdims=True)
+        gathered = jnp.dot(weights.astype(bf16), value_block, preferred_element_type=f32)
+        attended.append((gathered / total).astype(bf16))
+    attended_all[plane] = jnp.concatenate(attended, axis=1)
+
+    attended_copies = {}
+    for d in (2, 3, 1):
+        attended_copies[d] = remote(
+            attended_all.at[plane],
+            attended_all.at[plane],
+            attended_send.at[d],
+            attended_recv.at[d],
+            batch=flip(plane, d),
+        )
+        attended_copies[d].start()
+    for load in out_loads:
+        load.wait()
+    for d in others:
+        attended_copies[d].wait_recv()
+
+    def product(target):
+        return lax.dot_general(
+            attended_all[target],
+            w_out[...],
+            (((1,), (1,)), ((), ())),
+            preferred_element_type=f32,
+        )
+
+    core_copies = {}
+    for slot, mask in ((1, 3), (0, 1)):
+        core_out[slot] = product(flip(head, mask)).astype(bf16)
+        core_copies[slot] = remote(
+            core_out.at[slot],
+            core_in.at[slot],
+            core_send.at[slot],
+            core_recv.at[slot],
+            heads=flip(head, 1),
+        )
+        core_copies[slot].start()
+    far = product(flip(head, 2))
+    core_copies[1].wait_recv()
+    chip_out[...] = (far + core_in[1].astype(f32)).astype(bf16)
+    chip_copy = remote(chip_out, chip_in, chip_send, chip_recv, heads=flip(head, 2))
+    chip_copy.start()
+    near = product(head)
+    core_copies[0].wait_recv()
+    near = near + core_in[0].astype(f32)
+    chip_copy.wait_recv()
+    final[...] = (near + chip_in[...].astype(f32)).astype(bf16)
+
+    @pl.when(plane != head)
+    def _():
+        final_copy = remote(final, out, final_send, final_recv, batch=head, heads=plane)
+        final_copy.start()
+        final_copy.wait()
+
+    @pl.when(plane == head)
+    def _():
+        final_copy = pltpu.make_async_copy(final, out, final_send)
+        final_copy.start()
+        final_copy.wait()
+
+    for copies in (
+        token_copies,
+        share_copies,
+        key_copies,
+        value_copies,
+        segment_copies,
+        partial_copies,
+        attended_copies,
+        core_copies,
+    ):
+        for copy in copies.values():
+            copy.wait_send()
+    chip_copy.wait_send()
+
+
+SHARE = (1,)
+
+
+def move_activations(tokens, query_weight, keys, values, segment_ids, out_weight):
+    rows, model = tokens.shape
+    local_heads, depth, head_size = query_weight.shape
+    wide = local_heads * head_size
+    count = model // depth
+    bf16, dma = jnp.bfloat16, pltpu.SemaphoreType.DMA
+    anywhere = pl.BlockSpec(memory_space=pl.ANY)
+    scratch = [
+        pltpu.VMEM((depth, wide), bf16),
+        pltpu.VMEM((depth, wide), bf16),
+        pltpu.VMEM((count, rows, depth), bf16),
+        pltpu.VMEM((count, rows, wide), bf16),
+        pltpu.VMEM((count, rows, wide), bf16),
+        pltpu.VMEM((count, rows, head_size), bf16),
+        pltpu.VMEM((count, rows, head_size), bf16),
+        pltpu.VMEM((count, 8, 128), jnp.int32),
+        pltpu.VMEM((count, rows, wide), bf16),
+        pltpu.VMEM((2, rows, depth), bf16),
+        pltpu.VMEM((2, rows, depth), bf16),
+        pltpu.VMEM((rows, depth), bf16),
+        pltpu.VMEM((rows, depth), bf16),
+        pltpu.VMEM((rows, depth), bf16),
+        dma((3 + 2 * local_heads,)),
+        dma((count,)),
+        dma((count,)),
+        dma((count, len(SHARE))),
+        dma((count, len(SHARE))),
+        *[dma((count,)) for _ in range(10)],
+        dma((2,)),
+        dma((2,)),
+        *[dma for _ in range(4)],
+    ]
+    return pl.pallas_call(
+        kernel,
+        out_shape=jax.ShapeDtypeStruct((rows, depth), bf16),
+        in_specs=[
+            anywhere,
+            anywhere,
+            anywhere,
+            anywhere,
+            pl.BlockSpec(memory_space=pltpu.VMEM),
+            anywhere,
+        ],
+        out_specs=anywhere,
+        scratch_shapes=scratch,
+        compiler_params=pltpu.CompilerParams(
+            collective_id=0, has_side_effects=True, vmem_limit_bytes=32 * 1024 * 1024
+        ),
+        cost_estimate=pl.CostEstimate(
+            flops=4 * count * rows * depth * wide + 4 * local_heads * count * rows * rows * head_size,
+            bytes_accessed=4 * depth * wide + 4 * rows * model,
+            transcendentals=local_heads * count * rows * rows,
+        ),
+    )(tokens, query_weight, keys, values, segment_ids[None, :], out_weight)
+
+
+def gather_weights(tokens, query_weight, keys, values, segment_ids, out_weight):
     rows = tokens.shape[0]
     head_size = query_weight.shape[2]
     local_heads = query_weight.shape[0]
@@ -76,6 +452,17 @@
 
 
 def solution(mesh):
+    batch, heads = mesh.shape["batch"], mesh.shape["heads"]
+
+    def on_device(tokens, query_weight, keys, values, segment_ids, out_weight):
+        rows, model = tokens.shape
+        local_heads, depth, head_size = query_weight.shape
+        wide = local_heads * head_size
+        weights = 2 * model * wide
+        activations = batch * rows * (depth + 3 * wide + depth)
+        plan = move_activations if batch == heads == 4 and activations < weights else gather_weights
+        return plan(tokens, query_weight, keys, values, segment_ids, out_weight)
+
     return jax.shard_map(
         on_device,
         mesh=mesh,

time: 217 us -> 64.1 us (0.30); the launches traced: 214 us -> 63.7 us
  waiting for transfers between devices: 149 us -> 0 us
  Pallas kernels: 0 us -> 57.3 us
  blocking collectives: 37.3 us -> 0 us
  between operations: 13.8 us -> 0.02 us
  matrix products: 8.79 us -> 0 us
  local copies, waits for them, and re-layouts: 2.93 us -> 6.39 us
    all_gather x2 -> x0, waiting for transfers between devices: 122 us -> none  [the longest x1 76.7 us: on_device(): lax.all_gather(out_weight, 'batch', axis=1, tiled=True)]
    pallas_call x0 -> x1, Pallas kernels: none -> 57.3 us  [move_activations(): pl.pallas_call(kernel, out_shape=jax.ShapeDtypeStruct((rows, depth), bf16...]
    all_gather x2 -> x0, blocking collectives: 28.8 us -> none  [the longest x1 14.7 us: on_device(): value_piece = lax.all_gather(values, 'batch', axis=1, tiled=True)]
    reduce_scatter x1 -> x0, waiting for transfers between devices: 25.7 us -> none  [on_device(): lax.psum_scatter(terms, 'heads', scatter_dimension=1, tiled=True)]
    dot_general x4 -> x0, matrix products: 8.79 us -> none  [the longest x1 4.74 us: on_device(): jnp.einsum('htd,hcd->tc', attended, lax.all_gather(out_weight, 'batch', a...]
    unnamed x1 -> x0, blocking collectives: 8.44 us -> none
    unnamed x5 -> x13, local copies, waits for them, and re-layouts: 2.1 us -> 6.39 us
  transfers between devices with their start and end apart: 3 -> 0, of which waited for: 3 -> 0; matrix products, arithmetic and copies ran while one was open for 3% -> 0% of each run, Pallas kernels for 0% -> 0%
where the time goes in v1:
time: 64.1 us; the launch traced here: 63.7 us
  Pallas kernels  57.3 us (89%)
  local copies, waits for them, and re-layouts  6.39 us (10%)
    pallas_call x1, Pallas kernels, move_activations(): pl.pallas_call(kernel, out_shape=jax.ShapeDtypeStruct((rows, depth), bf16...  57.3 us
    unnamed x13, local copies, waits for them, and re-layouts  6.39 us

profile of v1, /device:TPU:2, one launch (start us, length us, event | category | flops | bytes accessed | tf_op | source)
XLA Modules:
  0.0 63.7 jit_solution(10811580808099769846)
XLA Ops:
  0.0 0.0 copy-start.5
  0.0 0.7 %copy-done.5 = s32[96]{0:T(128)S(1)} copy-done((s32[96]{0:T(128)S(1)}, s32[96]{0:T(128)}, u32[]{:S(2)}) %copy-start.5) | copy-done | bytes 408
  0.7 0.0 copy-start
  0.7 1.2 %copy-done = bf16[4,1024,128]{2,1,0:T(8,128)(2,1)S(1)} copy-done((bf16[4,1024,128]{2,1,0:T(8,128)(2,1)S(1)}, bf16[4,1024,128]{2,1,0:T(8,128)(2,1)}, u32[]{:S(2)}) %copy-start) | copy-done | bytes 1048600
  1.9 0.0 copy-start.1
  1.9 1.2 %copy-done.1 = bf16[4,1024,128]{2,1,0:T(8,128)(2,1)S(1)} copy-done((bf16[4,1024,128]{2,1,0:T(8,128)(2,1)S(1)}, bf16[4,1024,128]{2,1,0:T(8,128)(2,1)}, u32[]{:S(2)}) %copy-start.1) | copy-done | bytes 1048600
  3.1 0.0 copy-start.2
  3.1 1.1 %copy-done.2 = bf16[96,4096]{1,0:T(8,128)(2,1)S(1)} copy-done((bf16[96,4096]{1,0:T(8,128)(2,1)S(1)}, bf16[96,4096]{1,0:T(8,128)(2,1)}, u32[]{:S(2)}) %copy-start.2) | copy-done | bytes 786456
  4.2 0.0 copy-start.3
  4.2 0.7 %copy-done.3 = bf16[1,96,128]{2,1,0:T(8,128)(2,1)S(1)} copy-done((bf16[1,96,128]{2,1,0:T(8,128)(2,1)S(1)}, bf16[1,96,128]{2,1,0:T(8,128)(2,1)}, u32[]{:S(2)}) %copy-start.3) | copy-done | bytes 24600
  5.0 0.0 copy-start.4
  5.0 0.7 %copy-done.4 = bf16[1,96,128]{2,1,0:T(8,128)(2,1)S(1)} copy-done((bf16[1,96,128]{2,1,0:T(8,128)(2,1)S(1)}, bf16[1,96,128]{2,1,0:T(8,128)(2,1)}, u32[]{:S(2)}) %copy-start.4) | copy-done | bytes 24600
  5.7 57.3 %shard_map.64 = bf16[96,1024]{1,0:T(8,128)(2,1)S(1)} custom-call(bf16[96,4096]{1,0:T(8,128)(2,1)S(1)} %copy-done.2, bf16[4,1024,128]{2,1,0:T(8,128)(2,1)S(1)} %copy-done, bf16[1,96,128]{2,1,0:T(8,128)(2,1)S(1)} %copy-done.3, bf16[1,96,128]{2,1,0:T(8,128)(2,1)S(1)} %copy-done.4, s32[1,96]{1,0:T(1,128)S(1)} %bitcast.1, bf16[4,1024,128]{2,1,0:T(8,128)(2,1)S(1)} %copy-done.1), custom_call_target="tpu_custom_call" | custom-call | flops 880803840 | bytes 3670016 | tf_op jit(solution)/shard_map/pallas_call | solution.py:359
  63.0 0.7 %copy.8 = bf16[96,1024]{1,0:T(8,128)(2,1)} copy(bf16[96,1024]{1,0:T(8,128)(2,1)S(1)} %shard_map.64) | data formatting | bytes 393216
Async XLA Ops:
  0.0 0.7 %copy-start.5 = (s32[96]{0:T(128)S(1)}, s32[96]{0:T(128)}, u32[]{:S(2)}) copy-start(s32[96]{0:T(128)} %param.10) | copy-start | bytes 1156
  0.7 1.2 %copy-start = (bf16[4,1024,128]{2,1,0:T(8,128)(2,1)S(1)}, bf16[4,1024,128]{2,1,0:T(8,128)(2,1)}, u32[]{:S(2)}) copy-start(bf16[4,1024,128]{2,1,0:T(8,128)(2,1)} %query_weight.1) | copy-start | bytes 3145732
  1.9 1.2 %copy-start.1 = (bf16[4,1024,128]{2,1,0:T(8,128)(2,1)S(1)}, bf16[4,1024,128]{2,1,0:T(8,128)(2,1)}, u32[]{:S(2)}) copy-start(bf16[4,1024,128]{2,1,0:T(8,128)(2,1)} %out_weight.1) | copy-start | bytes 3145732
  3.1 1.1 %copy-start.2 = (bf16[96,4096]{1,0:T(8,128)(2,1)S(1)}, bf16[96,4096]{1,0:T(8,128)(2,1)}, u32[]{:S(2)}) copy-start(bf16[96,4096]{1,0:T(8,128)(2,1)} %tokens.1) | copy-start | bytes 2359300
  4.2 0.7 %copy-start.3 = (bf16[1,96,128]{2,1,0:T(8,128)(2,1)S(1)}, bf16[1,96,128]{2,1,0:T(8,128)(2,1)}, u32[]{:S(2)}) copy-start(bf16[1,96,128]{2,1,0:T(8,128)(2,1)} %keys.1) | copy-start | bytes 73732
  5.0 0.7 %copy-start.4 = (bf16[1,96,128]{2,1,0:T(8,128)(2,1)S(1)}, bf16[1,96,128]{2,1,0:T(8,128)(2,1)}, u32[]{:S(2)}) copy-start(bf16[1,96,128]{2,1,0:T(8,128)(2,1)} %values.1) | copy-start | bytes 73732

commit v2 on v1

--- a/solution.py
+++ b/solution.py
@@ -128,6 +128,22 @@
     share = depth // (1 + len(SHARE))
     my_share = lax.rem(head, 1 + len(SHARE))
     token_copies, share_copies, key_copies, value_copies, segment_copies = {}, {}, {}, {}, {}
+    partial_copies, attended_copies, core_copies = {}, {}, {}
+
+    def drain():
+        for copies in (
+            token_copies,
+            share_copies,
+            key_copies,
+            value_copies,
+            segment_copies,
+            partial_copies,
+            attended_copies,
+            core_copies,
+        ):
+            for copy in copies.values():
+                copy.wait_send()
+
     mine = pl.ds(pl.multiple_of(my_share * share, share), share)
     for d in (2, 3, 1):
         peer = flip(plane, d)
@@ -183,7 +199,6 @@
             )
             share_copies[d, s].start()
 
-    partial_copies = {}
     forward(1)
     forward(2)
     for d in others:
@@ -249,7 +264,6 @@
         attended.append((gathered / total).astype(bf16))
     attended_all[plane] = jnp.concatenate(attended, axis=1)
 
-    attended_copies = {}
     for d in (2, 3, 1):
         attended_copies[d] = remote(
             attended_all.at[plane],
@@ -272,7 +286,6 @@
             preferred_element_type=f32,
         )
 
-    core_copies = {}
     for slot, mask in ((1, 3), (0, 1)):
         core_out[slot] = product(flip(head, mask)).astype(bf16)
         core_copies[slot] = remote(
@@ -306,18 +319,7 @@
         final_copy.start()
         final_copy.wait()
 
-    for copies in (
-        token_copies,
-        share_copies,
-        key_copies,
-        value_copies,
-        segment_copies,
-        partial_copies,
-        attended_copies,
-        core_copies,
-    ):
-        for copy in copies.values():
-            copy.wait_send()
+    drain()
     chip_copy.wait_send()
 
 
@@ -330,7 +332,7 @@
     wide = local_heads * head_size
     count = model // depth
     bf16, dma = jnp.bfloat16, pltpu.SemaphoreType.DMA
-    anywhere = pl.BlockSpec(memory_space=pl.ANY)
+    anywhere = pl.BlockSpec(memory_space=pltpu.HBM)
     scratch = [
         pltpu.VMEM((depth, wide), bf16),
         pltpu.VMEM((depth, wide), bf16),
@@ -370,7 +372,7 @@
         out_specs=anywhere,
         scratch_shapes=scratch,
         compiler_params=pltpu.CompilerParams(
-            collective_id=0, has_side_effects=True, vmem_limit_bytes=32 * 1024 * 1024
+            collective_id=0, has_side_effects=True, vmem_limit_bytes=60 * 1024 * 1024
         ),
         cost_estimate=pl.CostEstimate(
             flops=4 * count * rows * depth * wide + 4 * local_heads * count * rows * rows * head_size,

time: 64.1 us -> 59.5 us (0.928)
  local copies, waits for them, and re-layouts: 6.39 us -> 1.62 us
    unnamed x13 -> x1, local copies, waits for them, and re-layouts: 6.39 us -> 1.62 us
where the time goes in v2:
time: 59.5 us; the launch traced here: 59.4 us
  Pallas kernels  57.8 us (97%)
  local copies, waits for them, and re-layouts  1.62 us (3%)
    pallas_call x1, Pallas kernels, move_activations(): pl.pallas_call(kernel, out_shape=jax.ShapeDtypeStruct((rows, depth), bf16...  57.8 us
    unnamed x1, local copies, waits for them, and re-layouts  1.62 us

profile of v2, /device:TPU:2, one launch (start us, length us, event | category | flops | bytes accessed | tf_op | source)
XLA Modules:
  0.0 59.4 jit_solution(7677012792172456775)
XLA Ops:
  0.0 57.8 %shard_map.64 = bf16[96,1024]{1,0:T(8,128)(2,1)} custom-call(bf16[96,4096]{1,0:T(8,128)(2,1)} %tokens.1, bf16[4,1024,128]{2,1,0:T(8,128)(2,1)} %query_weight.1, bf16[1,96,128]{2,1,0:T(8,128)(2,1)} %keys.1, bf16[1,96,128]{2,1,0:T(8,128)(2,1)} %values.1, s32[1,96]{1,0:T(1,128)} %bitcast.1, bf16[4,1024,128]{2,1,0:T(8,128)(2,1)} %out_weight.1), custom_call_target="tpu_custom_call" | custom-call | flops 880803840 | bytes 3670016 | tf_op jit(solution)/shard_map/pallas_call | solution.py:361
  57.8 1.6 %copy.8 = bf16[96,1024]{1,0:T(8,128)(2,1)} copy(bf16[96,1024]{1,0:T(8,128)(2,1)} %shard_map.64) | data formatting | bytes 393216

commit v3 on v2

--- a/solution.py
+++ b/solution.py
@@ -114,21 +114,24 @@
         )
         pl.semaphore_signal(barrier, inc=1, device_id={"heads": flip(head, d)}, device_id_type=MESH)
 
-    @pl.when(plane != head)
+    target, origin = rows_of(head), rows_of(plane)
+    stays = (plane == head) & (target == head)
+
+    @pl.when(jnp.logical_not(stays))
     def _():
         pl.semaphore_signal(
-            barrier, inc=1, device_id={"batch": head, "heads": plane}, device_id_type=MESH
+            barrier, inc=1, device_id={"batch": head, "heads": origin}, device_id_type=MESH
         )
         pl.semaphore_wait(barrier, 2 * len(others) + 1)
 
-    @pl.when(plane == head)
+    @pl.when(stays)
     def _():
         pl.semaphore_wait(barrier, 2 * len(others))
 
     share = depth // (1 + len(SHARE))
     my_share = lax.rem(head, 1 + len(SHARE))
     token_copies, share_copies, key_copies, value_copies, segment_copies = {}, {}, {}, {}, {}
-    partial_copies, attended_copies, core_copies = {}, {}, {}
+    partial_copies, attended_copies, core_copies, chip_copies = {}, {}, {}, {}
 
     def drain():
         for copies in (
@@ -140,6 +143,7 @@
             partial_copies,
             attended_copies,
             core_copies,
+            chip_copies,
         ):
             for copy in copies.values():
                 copy.wait_send()
@@ -182,6 +186,7 @@
             for copy in (key_copies[d], value_copies[d], segment_copies[d]):
                 copy.start()
 
+    send_keys()
     for load in query_loads:
         load.wait()
     own_tokens.wait()
@@ -217,8 +222,6 @@
             batch=flip(plane, d),
         )
         partial_copies[d].start()
-        if d == 1:
-            send_keys()
 
     for d in others:
         segment_copies[d].wait_recv()
@@ -287,7 +290,7 @@
         )
 
     for slot, mask in ((1, 3), (0, 1)):
-        core_out[slot] = product(flip(head, mask)).astype(bf16)
+        core_out[slot] = product(rows_of(flip(head, mask))).astype(bf16)
         core_copies[slot] = remote(
             core_out.at[slot],
             core_in.at[slot],
@@ -296,34 +299,58 @@
             heads=flip(head, 1),
         )
         core_copies[slot].start()
-    far = product(flip(head, 2))
+    far = product(rows_of(flip(head, 2)))
+    width = depth // PIECES
+    parts = [pl.ds(p * width, width) for p in range(PIECES)]
     core_copies[1].wait_recv()
-    chip_out[...] = (far + core_in[1].astype(f32)).astype(bf16)
-    chip_copy = remote(chip_out, chip_in, chip_send, chip_recv, heads=flip(head, 2))
-    chip_copy.start()
-    near = product(head)
+    for p, part in enumerate(parts):
+        chip_out[p] = (far[:, p * width : (p + 1) * width] + core_in[1, :, part].astype(f32)).astype(
+            bf16
+        )
+        chip_copies[p] = remote(
+            chip_out.at[p],
+            chip_in.at[p],
+            chip_send.at[p],
+            chip_recv.at[p],
+            heads=flip(head, 2),
+        )
+        chip_copies[p].start()
+    near = product(target)
     core_copies[0].wait_recv()
     near = near + core_in[0].astype(f32)
-    chip_copy.wait_recv()
-    final[...] = (near + chip_in[...].astype(f32)).astype(bf16)
-
-    @pl.when(plane != head)
-    def _():
-        final_copy = remote(final, out, final_send, final_recv, batch=head, heads=plane)
-        final_copy.start()
-        final_copy.wait()
-
-    @pl.when(plane == head)
-    def _():
-        final_copy = pltpu.make_async_copy(final, out, final_send)
-        final_copy.start()
-        final_copy.wait()
+    for p, part in enumerate(parts):
+        chip_copies[p].wait_recv()
+        final[p] = (near[:, p * width : (p + 1) * width] + chip_in[p].astype(f32)).astype(bf16)
+        send = (final.at[p], out.at[:, part], final_send.at[p])
+
+        @pl.when(jnp.logical_not(stays))
+        def _():
+            remote(*send, final_recv.at[p], batch=target, heads=plane).start()
+
+        @pl.when(stays)
+        def _():
+            pltpu.make_async_copy(*send).start()
+
+    for p, part in enumerate(parts):
+        send = (final.at[p], out.at[:, part], final_send.at[p])
+
+        @pl.when(jnp.logical_not(stays))
+        def _():
+            remote(*send, final_recv.at[p], batch=target, heads=plane).wait()
+
+        @pl.when(stays)
+        def _():
+            pltpu.make_async_copy(*send).wait()
 
     drain()
-    chip_copy.wait_send()
-
-
-SHARE = (1,)
+
+
+SHARE = (1, 2, 3)
+PIECES = 4
+
+
+def rows_of(index):
+    return 2 * lax.rem(index, 2) + lax.div(index, 2)
 
 
 def move_activations(tokens, query_weight, keys, values, segment_ids, out_weight):
@@ -345,9 +372,9 @@
         pltpu.VMEM((count, rows, wide), bf16),
         pltpu.VMEM((2, rows, depth), bf16),
         pltpu.VMEM((2, rows, depth), bf16),
-        pltpu.VMEM((rows, depth), bf16),
-        pltpu.VMEM((rows, depth), bf16),
-        pltpu.VMEM((rows, depth), bf16),
+        pltpu.VMEM((PIECES, rows, depth // PIECES), bf16),
+        pltpu.VMEM((PIECES, rows, depth // PIECES), bf16),
+        pltpu.VMEM((PIECES, rows, depth // PIECES), bf16),
         dma((3 + 2 * local_heads,)),
         dma((count,)),
         dma((count,)),
@@ -356,7 +383,7 @@
         *[dma((count,)) for _ in range(10)],
         dma((2,)),
         dma((2,)),
-        *[dma for _ in range(4)],
+        *[dma((PIECES,)) for _ in range(4)],
     ]
     return pl.pallas_call(
         kernel,

time: 59.5 us -> 52.8 us (0.89)
  the two profiles are of different devices: /device:TPU:2 before, /device:TPU:1 now
where the time goes in v3:
time: 52.8 us; the launch traced here: 52.7 us
  Pallas kernels  51.1 us (97%)
  local copies, waits for them, and re-layouts  1.62 us (3%)
    pallas_call x1, Pallas kernels, move_activations(): pl.pallas_call(kernel, out_shape=jax.ShapeDtypeStruct((rows, depth), bf16...  51.1 us
    unnamed x1, local copies, waits for them, and re-layouts  1.62 us

profile of v3, /device:TPU:1, one launch (start us, length us, event | category | flops | bytes accessed | tf_op | source)
XLA Modules:
  0.0 52.7 jit_solution(16383728445538699038)
XLA Ops:
  0.0 51.1 %shard_map.64 = bf16[96,1024]{1,0:T(8,128)(2,1)} custom-call(bf16[96,4096]{1,0:T(8,128)(2,1)} %tokens.1, bf16[4,1024,128]{2,1,0:T(8,128)(2,1)} %query_weight.1, bf16[1,96,128]{2,1,0:T(8,128)(2,1)} %keys.1, bf16[1,96,128]{2,1,0:T(8,128)(2,1)} %values.1, s32[1,96]{1,0:T(1,128)} %bitcast.1, bf16[4,1024,128]{2,1,0:T(8,128)(2,1)} %out_weight.1), custom_call_target="tpu_custom_call" | custom-call | flops 880803840 | bytes 3670016 | tf_op jit(solution)/shard_map/pallas_call | solution.py:388
  51.1 1.6 %copy.8 = bf16[96,1024]{1,0:T(8,128)(2,1)} copy(bf16[96,1024]{1,0:T(8,128)(2,1)} %shard_map.64) | data formatting | bytes 393216

commit v4 on v3

--- a/solution.py
+++ b/solution.py
@@ -41,6 +41,7 @@
     chip_out,
     chip_in,
     final,
+    kept,
     load_sem,
     token_send,
     token_recv,
@@ -69,6 +70,7 @@
     plane = lax.axis_index("batch")
     head = lax.axis_index("heads")
     others = (1, 2, 3)
+    head_columns = [pl.ds(i * head_size, head_size) for i in range(local_heads)]
     bf16, f32 = jnp.bfloat16, jnp.float32
 
     def remote(src, dst, send, recv, **device):
@@ -214,14 +216,15 @@
         partial_out[d] = jnp.dot(token_block[d], w_query[...], preferred_element_type=f32).astype(
             bf16
         )
-        partial_copies[d] = remote(
-            partial_out.at[d],
-            partial_in.at[d],
-            partial_send.at[d],
-            partial_recv.at[d],
-            batch=flip(plane, d),
-        )
-        partial_copies[d].start()
+        for i, columns in enumerate(head_columns):
+            partial_copies[d, i] = remote(
+                partial_out.at[d, :, columns],
+                partial_in.at[d, :, columns],
+                partial_send.at[d, i],
+                partial_recv.at[d, i],
+                batch=flip(plane, d),
+            )
+            partial_copies[d, i].start()
 
     for d in others:
         segment_copies[d].wait_recv()
@@ -244,16 +247,15 @@
         value_copies[d].wait_recv()
     key_block = jnp.concatenate([key_all[p] for p in range(count)], axis=0)
     value_block = jnp.concatenate([value_all[p] for p in range(count)], axis=0)
-    for d in others:
-        partial_copies[d].wait_recv()
-        query = query + partial_in[d].astype(f32)
-    query = query.astype(bf16)
     factor = 1.0 / (head_size**0.5)
-    attended = []
-    for i in range(local_heads):
+    for i, columns in enumerate(head_columns):
+        head_query = query[:, i * head_size : (i + 1) * head_size]
+        for d in others:
+            partial_copies[d, i].wait_recv()
+            head_query = head_query + partial_in[d, :, columns].astype(f32)
         scores = (
             lax.dot_general(
-                query[:, i * head_size : (i + 1) * head_size],
+                head_query.astype(bf16),
                 key_block,
                 (((1,), (1,)), ((), ())),
                 preferred_element_type=f32,
@@ -264,22 +266,18 @@
         weights = jnp.where(keep, jnp.exp(scores - top), 0.0)
         total = jnp.sum(weights, axis=1, keepdims=True)
         gathered = jnp.dot(weights.astype(bf16), value_block, preferred_element_type=f32)
-        attended.append((gathered / total).astype(bf16))
-    attended_all[plane] = jnp.concatenate(attended, axis=1)
-
-    for d in (2, 3, 1):
-        attended_copies[d] = remote(
-            attended_all.at[plane],
-            attended_all.at[plane],
-            attended_send.at[d],
-            attended_recv.at[d],
-            batch=flip(plane, d),
-        )
-        attended_copies[d].start()
+        attended_all[plane, :, columns] = (gathered / total).astype(bf16)
+        for d in (2, 3, 1):
+            attended_copies[d, i] = remote(
+                attended_all.at[plane, :, columns],
+                attended_all.at[plane, :, columns],
+                attended_send.at[d, i],
+                attended_recv.at[d, i],
+                batch=flip(plane, d),
+            )
+            attended_copies[d, i].start()
     for load in out_loads:
         load.wait()
-    for d in others:
-        attended_copies[d].wait_recv()
 
     def product(target):
         return lax.dot_general(
@@ -289,8 +287,7 @@
             preferred_element_type=f32,
         )
 
-    for slot, mask in ((1, 3), (0, 1)):
-        core_out[slot] = product(rows_of(flip(head, mask))).astype(bf16)
+    for slot in range(2):
         core_copies[slot] = remote(
             core_out.at[slot],
             core_in.at[slot],
@@ -298,13 +295,32 @@
             core_recv.at[slot],
             heads=flip(head, 1),
         )
-        core_copies[slot].start()
-    far = product(rows_of(flip(head, 2)))
+    for d in (0, *others):
+        if d:
+            for i in range(local_heads):
+                attended_copies[d, i].wait_recv()
+        rows_at = flip(plane, d)
+        adder = rows_of(rows_at)
+        term = product(rows_at)
+        here = lax.rem(adder, 2) == lax.rem(head, 2)
+        for slot in range(2):
+            same = lax.div(adder, 2) == lax.div(head, 2)
+            this = same if slot == 0 else jnp.logical_not(same)
+
+            @pl.when(here & this)
+            def _():
+                kept[slot] = term
+
+            @pl.when(jnp.logical_not(here) & this)
+            def _():
+                core_out[slot] = term.astype(bf16)
+                core_copies[slot].start()
+
     width = depth // PIECES
     parts = [pl.ds(p * width, width) for p in range(PIECES)]
     core_copies[1].wait_recv()
     for p, part in enumerate(parts):
-        chip_out[p] = (far[:, p * width : (p + 1) * width] + core_in[1, :, part].astype(f32)).astype(
+        chip_out[p] = (kept[1, :, part] + core_in[1, :, part].astype(f32)).astype(
             bf16
         )
         chip_copies[p] = remote(
@@ -315,9 +331,8 @@
             heads=flip(head, 2),
         )
         chip_copies[p].start()
-    near = product(target)
     core_copies[0].wait_recv()
-    near = near + core_in[0].astype(f32)
+    near = kept[0] + core_in[0].astype(f32)
     for p, part in enumerate(parts):
         chip_copies[p].wait_recv()
         final[p] = (near[:, p * width : (p + 1) * width] + chip_in[p].astype(f32)).astype(bf16)
@@ -375,12 +390,14 @@
         pltpu.VMEM((PIECES, rows, depth // PIECES), bf16),
         pltpu.VMEM((PIECES, rows, depth // PIECES), bf16),
         pltpu.VMEM((PIECES, rows, depth // PIECES), bf16),
+        pltpu.VMEM((2, rows, depth), jnp.float32),
         dma((3 + 2 * local_heads,)),
         dma((count,)),
         dma((count,)),
         dma((count, len(SHARE))),
         dma((count, len(SHARE))),
-        *[dma((count,)) for _ in range(10)],
+        *[dma((count,)) for _ in range(6)],
+        *[dma((count, local_heads)) for _ in range(4)],
         dma((2,)),
         dma((2,)),
         *[dma((PIECES,)) for _ in range(4)],

time: 52.8 us -> 50.3 us (0.953)
  Pallas kernels: 51.1 us -> 48.6 us
    pallas_call x1, Pallas kernels: 51.1 us -> 48.6 us  [move_activations(): pl.pallas_call(kernel, out_shape=jax.ShapeDtypeStruct((rows, depth), bf16...]
where the time goes in v4:
time: 50.3 us; the launch traced here: 50.2 us
  Pallas kernels  48.6 us (97%)
  local copies, waits for them, and re-layouts  1.62 us (3%)
    pallas_call x1, Pallas kernels, move_activations(): pl.pallas_call(kernel, out_shape=jax.ShapeDtypeStruct((rows, depth), bf16...  48.6 us
    unnamed x1, local copies, waits for them, and re-layouts  1.62 us

profile of v4, /device:TPU:1, one launch (start us, length us, event | category | flops | bytes accessed | tf_op | source)
XLA Modules:
  0.0 50.2 jit_solution(2277146651695442128)
XLA Ops:
  0.0 48.6 %shard_map.64 = bf16[96,1024]{1,0:T(8,128)(2,1)} custom-call(bf16[96,4096]{1,0:T(8,128)(2,1)} %tokens.1, bf16[4,1024,128]{2,1,0:T(8,128)(2,1)} %query_weight.1, bf16[1,96,128]{2,1,0:T(8,128)(2,1)} %keys.1, bf16[1,96,128]{2,1,0:T(8,128)(2,1)} %values.1, s32[1,96]{1,0:T(1,128)} %bitcast.1, bf16[4,1024,128]{2,1,0:T(8,128)(2,1)} %out_weight.1), custom_call_target="tpu_custom_call" | custom-call | flops 880803840 | bytes 3670016 | tf_op jit(solution)/shard_map/pallas_call | solution.py:405
  48.6 1.6 %copy.8 = bf16[96,1024]{1,0:T(8,128)(2,1)} copy(bf16[96,1024]{1,0:T(8,128)(2,1)} %shard_map.64) | data formatting | bytes 393216

commit v5 on v4

--- a/solution.py
+++ b/solution.py
@@ -192,7 +192,6 @@
     for load in query_loads:
         load.wait()
     own_tokens.wait()
-    query = jnp.dot(token_block[0], w_query[...], preferred_element_type=f32)
 
     def forward(d):
         token_copies[d].wait_recv()
@@ -208,6 +207,7 @@
 
     forward(1)
     forward(2)
+    query = jnp.dot(token_block[0], w_query[...], preferred_element_type=f32)
     for d in others:
         for s in range(len(SHARE)):
             share_copies[d, s].wait_recv()
@@ -295,6 +295,25 @@
             core_recv.at[slot],
             heads=flip(head, 1),
         )
+    width = depth // PIECES
+    parts = [pl.ds(p * width, width) for p in range(PIECES)]
+    for p in range(PIECES):
+        chip_copies[p] = remote(
+            chip_out.at[p],
+            chip_in.at[p],
+            chip_send.at[p],
+            chip_recv.at[p],
+            heads=flip(head, 2),
+        )
+
+    def send_chip(d):
+        @pl.when(rows_of(flip(plane, d)) == flip(head, 2))
+        def _():
+            core_copies[1].wait_recv()
+            for p, part in enumerate(parts):
+                chip_out[p] = (kept[1, :, part] + core_in[1, :, part].astype(f32)).astype(bf16)
+                chip_copies[p].start()
+
     for d in (0, *others):
         if d:
             for i in range(local_heads):
@@ -316,21 +335,9 @@
                 core_out[slot] = term.astype(bf16)
                 core_copies[slot].start()
 
-    width = depth // PIECES
-    parts = [pl.ds(p * width, width) for p in range(PIECES)]
-    core_copies[1].wait_recv()
-    for p, part in enumerate(parts):
-        chip_out[p] = (kept[1, :, part] + core_in[1, :, part].astype(f32)).astype(
-            bf16
-        )
-        chip_copies[p] = remote(
-            chip_out.at[p],
-            chip_in.at[p],
-            chip_send.at[p],
-            chip_recv.at[p],
-            heads=flip(head, 2),
-        )
-        chip_copies[p].start()
+        if d:
+            send_chip(d - 1)
+    send_chip(others[-1])
     core_copies[0].wait_recv()
     near = kept[0] + core_in[0].astype(f32)
     for p, part in enumerate(parts):

time: 50.3 us -> 49.7 us (0.988)
  the two profiles are of different devices: /device:TPU:1 before, /device:TPU:24 now
where the time goes in v5:
time: 49.7 us; the launch traced here: 49.5 us
  Pallas kernels  47.9 us (96%)
  local copies, waits for them, and re-layouts  1.62 us (3%)
    pallas_call x1, Pallas kernels, move_activations(): pl.pallas_call(kernel, out_shape=jax.ShapeDtypeStruct((rows, depth), bf16...  47.9 us
    unnamed x1, local copies, waits for them, and re-layouts  1.62 us

profile of v5, /device:TPU:24, one launch (start us, length us, event | category | flops | bytes accessed | tf_op | source)
XLA Modules:
  0.0 49.5 jit_solution(17504377102934839986)
XLA Ops:
  0.0 47.9 %shard_map.64 = bf16[96,1024]{1,0:T(8,128)(2,1)} custom-call(bf16[96,4096]{1,0:T(8,128)(2,1)} %tokens.1, bf16[4,1024,128]{2,1,0:T(8,128)(2,1)} %query_weight.1, bf16[1,96,128]{2,1,0:T(8,128)(2,1)} %keys.1, bf16[1,96,128]{2,1,0:T(8,128)(2,1)} %values.1, s32[1,96]{1,0:T(1,128)} %bitcast.1, bf16[4,1024,128]{2,1,0:T(8,128)(2,1)} %out_weight.1), custom_call_target="tpu_custom_call" | custom-call | flops 880803840 | bytes 3670016 | tf_op jit(solution)/shard_map/pallas_call | solution.py:412
  47.9 1.6 %copy.8 = bf16[96,1024]{1,0:T(8,128)(2,1)} copy(bf16[96,1024]{1,0:T(8,128)(2,1)} %shard_map.64) | data formatting | bytes 393216
